TPU v7x, 32 devices: a whole 2x2x4 slice. The times are simulated.
32 devices in a mesh: groups: 2 (over x), vel: 8 (over z, y), sub: 2 (over core).
Axes of the slice: x: 2, y: 2, z: 4, core: 2. Of those that a mesh axis runs over, the one named last changes fastest.
Arguments:
- dist: float32 [16, 256, 1024], P('sub', 'vel', 'groups'), parts along dimension 2, may hold values from 0 to 6, as said below
- cell_type: int32 [1024], P('groups'), parts along dimension 0, may hold values from 0 to 1, as said below
- groove_mask: int32 [64], P('groups'), parts along dimension 0, may hold values 0 or 1
Outputs:
- dist_next: float32 [16, 256, 1024], P('sub', 'vel', 'groups'), parts along dimension 2
There are 2 independent parts, one for each index of `groups`. A program takes and returns all parts, laid end to end along the dimension named above; each array names one. Nothing has to cross between parts.
Inputs may be any that keep to these rules, and one draw needn't show every extreme that they name: `cell_type`: in each column the solid cells are its lowest ones; a column holds at most a quarter of 16 of them, and every draw has columns with that many and columns with none; grooves repeat along the columns with a period of 4 to 12 columns. `dist`: every entry is positive.
All inputs are finite; a program needn't handle non-finite values.
Results may differ from a plain program's by a relative error of at most 0.0001.
Values sent between devices are 32-bit elements; how exact they have to be, the bound alone decides.
A program may use at most 128 MiB of HBM per device.

v0:
```python
import math
import jax
import jax.numpy as jnp
from jax import lax
from jax.sharding import PartitionSpec as P

VN = 16
SY = 16
STEPS = 2
VEL_RANGE = 5.0
TOP_SPEED = 1.0
ACC_LAND = 0.4
ACC_TOP = 0.7
KNUDSEN = 1.0
HIGHEST = lax.Precision.HIGHEST
FORMS = ("kj,jxzc->kxzc", "kj,yjzc->ykzc", "kj,yxjc->yxkc")


def swapped(value, axis, distance):
    mask = 2**distance
    pairs = [(source, source ^ mask) for source in range(lax.axis_size(axis))]
    return lax.ppermute(value, axis, pairs)


def spacing_of(count):
    return 2.0 * VEL_RANGE / count


def time_step(count):
    return 0.8 / ((count - 1) * spacing_of(count))


def speeds(index, count):
    return (index.astype(jnp.float32) - (count - 1) / 2.0) * spacing_of(count)


def wave_numbers(count):
    index = jnp.arange(count, dtype=jnp.int32)
    wrapped = jnp.where(index < count // 2, index, index - count)
    return wrapped.astype(jnp.float32) * (math.pi / VEL_RANGE)


def kernels(count):
    wave = wave_numbers(count)
    wave_y = wave[:, None, None]
    wave_x = wave[None, :, None]
    wave_z = wave[None, None, :]
    square = wave_y * wave_y + wave_x * wave_x + wave_z * wave_z
    first = 1.0 / (1.0 + square / 12.0)
    second = 3.0 * jnp.cos(0.9 * wave_x) / (1.0 + square / 10.0)
    damped = 1.0 + square / 9.0
    loss = 3.0 / (damped * damped)
    return (first, second, loss)


def dft_tables(count):
    index = jnp.arange(count, dtype=jnp.float32)
    angle = 2.0 * math.pi / count * index[:, None] * index[None, :]
    return (jnp.cos(angle), jnp.sin(angle))


def full_grid(count):
    index = jnp.arange(count * count * count, dtype=jnp.int32)
    velocity_y = speeds(index // (count * count), count)
    velocity_x = speeds(index // count % count, count)
    velocity_z = speeds(index % count, count)
    return (velocity_x, velocity_y, velocity_z)


def wall_tables(velocity_x, velocity_y, velocity_z):
    rest = jnp.exp(
        -(velocity_x * velocity_x + velocity_y * velocity_y + velocity_z * velocity_z) / 2.0
    )
    shifted = velocity_x - TOP_SPEED
    moving = jnp.exp(-(shifted * shifted + velocity_y * velocity_y + velocity_z * velocity_z) / 2.0)
    weights = jnp.stack(
        [
            jnp.maximum(-velocity_x, 0.0),
            jnp.maximum(velocity_x, 0.0),
            jnp.maximum(-velocity_y, 0.0),
            jnp.maximum(velocity_y, 0.0),
        ]
    )
    return (rest, moving, weights)


def wall_norms(count):
    velocity_x, velocity_y, velocity_z = full_grid(count)
    rest, moving, weights = wall_tables(velocity_x, velocity_y, velocity_z)
    return (
        jnp.sum(jnp.maximum(velocity_x, 0.0) * rest),
        jnp.sum(jnp.maximum(-velocity_x, 0.0) * rest),
        jnp.sum(jnp.maximum(velocity_y, 0.0) * rest),
        jnp.sum(jnp.maximum(-velocity_y, 0.0) * moving),
    )


def cell_masks(cell_type, groove_mask, height_count):
    total = cell_type.shape[0]
    solid = cell_type.astype(jnp.float32)
    height = jnp.arange(total, dtype=jnp.int32) % height_count
    left_solid = jnp.roll(solid, height_count)
    right_solid = jnp.roll(solid, -height_count)
    below_solid = jnp.where(height == 0, 1.0, jnp.roll(solid, 1))
    top_wall = jnp.where(height == height_count - 1, 1.0, 0.0 * solid)
    accommodation = jnp.repeat(jnp.where(groove_mask == 1, 1.0, ACC_LAND), height_count)
    return jnp.stack([left_solid, right_solid, below_solid, top_wall, accommodation, 1.0 - solid])


def advance(center, left, right, below, above, mirror, flux, masks, velocity, norms, step_size):
    velocity_x, velocity_y, rest, moving = velocity
    left_solid = masks[0][None, :]
    right_solid = masks[1][None, :]
    below_solid = masks[2][None, :]
    top_wall = masks[3][None, :]
    accommodation = masks[4][None, :]
    fluid = masks[5][None, :]
    left_ghost = (flux[0] / norms[0])[None, :] * rest
    right_ghost = (flux[1] / norms[1])[None, :] * rest
    below_ghost = (1.0 - accommodation) * mirror + accommodation * (flux[2] / norms[2])[
        None, :
    ] * rest
    above_ghost = (1.0 - ACC_TOP) * mirror + ACC_TOP * (flux[3] / norms[3])[None, :] * moving
    left_value = jnp.where(left_solid > 0.0, left_ghost, left)
    right_value = jnp.where(right_solid > 0.0, right_ghost, right)
    below_value = jnp.where(below_solid > 0.0, below_ghost, below)
    above_value = jnp.where(top_wall > 0.0, above_ghost, above)
    change = jnp.maximum(velocity_x, 0.0) * (center - left_value) + jnp.minimum(velocity_x, 0.0) * (
        right_value - center
    )
    change = (
        change
        + jnp.maximum(velocity_y, 0.0) * (center - below_value)
        + jnp.minimum(velocity_y, 0.0) * (above_value - center)
    )
    return (center - step_size * change) * fluid


def fourier_pass(real_part, imag_part, cosine, sine_table, form, forward):

    def apply(table, values):
        return jnp.einsum(form, table, values, precision=HIGHEST)

    if imag_part is None:
        return (apply(cosine, real_part), -apply(sine_table, real_part))
    if forward:
        return (
            apply(cosine, real_part) + apply(sine_table, imag_part),
            apply(cosine, imag_part) - apply(sine_table, real_part),
        )
    return (
        apply(cosine, real_part) - apply(sine_table, imag_part),
        apply(cosine, imag_part) + apply(sine_table, real_part),
    )


def collide(cube, tables, cosine, sine_table, rate):
    count = cube.shape[0]
    scale = 1.0 / (count * count * count)
    real_part, imag_part = fourier_pass(cube, None, cosine, sine_table, FORMS[0], True)
    real_part, imag_part = fourier_pass(real_part, imag_part, cosine, sine_table, FORMS[1], True)
    real_part, imag_part = fourier_pass(real_part, imag_part, cosine, sine_table, FORMS[2], True)

    def inverse(table):
        factor = table[..., None]
        first_real, first_imag = fourier_pass(
            real_part * factor, imag_part * factor, cosine, sine_table, FORMS[0], False
        )
        second_real, second_imag = fourier_pass(
            first_real, first_imag, cosine, sine_table, FORMS[1], False
        )
        last = jnp.einsum(FORMS[2], cosine, second_real, precision=HIGHEST) - jnp.einsum(
            FORMS[2], sine_table, second_imag, precision=HIGHEST
        )
        return last * scale

    gain = inverse(tables[0]) * inverse(tables[1])
    return cube + rate * (gain - cube * inverse(tables[2]))


def local(dist, cell_type, groove_mask):
    count = VN
    height_count = SY
    volume = count * count * count
    local_y, local_xz, total_cells = dist.shape
    masks = cell_masks(cell_type, groove_mask, height_count)
    norms = wall_norms(count)
    step_size = time_step(count)
    rate = step_size / KNUDSEN
    cosine, sine_table = dft_tables(count)
    tables = kernels(count)
    sub_index = lax.axis_index("sub")
    vel_index = lax.axis_index("vel")
    index_y = sub_index * local_y + jnp.arange(local_y, dtype=jnp.int32)
    index_xz = vel_index * local_xz + jnp.arange(local_xz, dtype=jnp.int32)
    block_shape = (local_y, local_xz)
    velocity_y = jnp.broadcast_to(speeds(index_y, count)[:, None], block_shape).reshape(-1)
    velocity_x = jnp.broadcast_to(speeds(index_xz // count, count)[None, :], block_shape).reshape(
        -1
    )
    velocity_z = jnp.broadcast_to(speeds(index_xz % count, count)[None, :], block_shape).reshape(-1)
    rest, moving, weights = wall_tables(velocity_x, velocity_y, velocity_z)
    velocity = (velocity_x[:, None], velocity_y[:, None], rest[:, None], moving[:, None])
    columns_total = total_cells // height_count
    depth = jnp.sum(cell_type.reshape(columns_total, height_count), axis=1)
    bottom_index = jnp.arange(columns_total, dtype=jnp.int32) * height_count + depth
    state = dist
    for iteration in range(STEPS):
        space = lax.all_to_all(
            lax.all_to_all(state, "vel", split_axis=2, concat_axis=1, tiled=True),
            "sub",
            split_axis=2,
            concat_axis=0,
            tiled=True,
        )
        cells = space.shape[2]
        post = collide(
            space.reshape(count, count, count, cells), tables, cosine, sine_table, rate
        ).reshape(volume, cells)
        back = lax.all_to_all(
            lax.all_to_all(
                post.reshape(count, count * count, 1, cells),
                "vel",
                split_axis=1,
                concat_axis=2,
                tiled=True,
            ),
            "sub",
            split_axis=0,
            concat_axis=3,
            tiled=True,
        )
        center = back.reshape(local_y * local_xz, total_cells)
        flux = lax.psum(jnp.dot(weights, center, precision=HIGHEST), ("vel", "sub"))
        shaped = center.reshape(local_y, local_xz, total_cells)
        bottom_rows = jnp.take(shaped, bottom_index, axis=2)
        top_rows = shaped[:, :, height_count - 1 :: height_count]
        outgoing = jnp.where(sub_index == 0, bottom_rows, top_rows)
        incoming = swapped(outgoing, "sub", 0)
        mirror = jnp.repeat(incoming[::-1], height_count, axis=2).reshape(
            local_y * local_xz, total_cells
        )
        result = advance(
            center,
            jnp.roll(center, height_count, 1),
            jnp.roll(center, -height_count, 1),
            jnp.roll(center, 1, 1),
            jnp.roll(center, -1, 1),
            mirror,
            flux,
            masks,
            velocity,
            norms,
            step_size,
        )
        state = result.reshape(local_y, local_xz, total_cells)
    return state


def solution(mesh):
    return jax.shard_map(
        local,
        mesh=mesh,
        in_specs=(P("sub", "vel", "groups"), P("groups"), P("groups")),
        out_specs=P("sub", "vel", "groups"),
        check_vma=False,
    )
```

profile of v0, /device:TPU:1, one launch (start us, length us, event | category | flops | bytes accessed | tf_op | source)
XLA Modules:
  0.0 529.2 jit_solution(7535001363961206787)
XLA Ops:
  3.6 6.4 %all-to-all-start = ((f32[8,1,16384]{2,1,0:T(1,128)}), f32[8,1,16384]{2,1,0:T(1,128)S(1)}, u32[]{:S(2)}, u32[]{:S(2)}) async-start(f32[8,1,16384]{2,1,0:T(1,128)} %reshape.613), calls=%async_computation | async-start | bytes 1048576 | tf_op jit(solution)/shard_map/all_to_all | solution.py:210
  19.5 3.9 all-to-all-done
  27.4 5.8 %all_to_all.132 = f32[8,256,64]{1,0,2:T(8,128)S(1)} all-to-all(f32[8,256,64]{1,0,2:T(8,128)S(1)} %copy.780), channel_id=1, replica_groups=mesh['groups'=2,'vel'=8,'sub'=2] {'sub'}, dimensions={2} | all-to-all | bytes 1048576 | tf_op jit(solution)/shard_map/all_to_all | solution.py:209
  45.2 3.5 subtract_bitcast_fusion.7
  91.4 3.7 fusion.104
  103.9 3.5 fusion.118
  117.1 3.5 add_bitcast_fusion.6
  128.6 3.8 subtract_bitcast_fusion.4
  155.9 8.6 %fusion.5 = f32[16,16,16,32]{3,0,2,1:T(8,128)} fusion(f32[16,16,16,32]{3,0,2,1:T(8,128)S(1)} %bitcast.348, f32[16,16,32,16]{2,3,1,0:T(8,128)S(1)} %fusion.23, f32[16,16,32,16]{2,3,1,0:T(8,128)S(1)} %fusion.25, f32[16,16,32,16]{2,3,1,0:T(8,128)S(1)} %fusion.29, f32[16,16,32,16]{2,3,1,0:T(8,128)S(1)} %fusion.31, f32[16,16,32,16]{2,3,1,0:T(8,128)S(1)} %fusion.34, ...), kind=kLoop, calls=%fused_computation.9 | loop fusion | flops 1441792 | bytes 4194304 | tf_op jit(solution)/shard_map/add | solution.py:178
  167.7 3.9 all-to-all-start.2
  177.5 7.6 %all-to-all-done.2 = f32[8,1,16384]{2,1,0:T(1,128)S(1)} async-done(((f32[8,1,16384]{2,1,0:T(1,128)}), f32[8,1,16384]{2,1,0:T(1,128)S(1)}, u32[]{:S(2)}, u32[]{:S(2)}) %all-to-all-start.2) | async-done | bytes 524320 | tf_op jit(solution)/shard_map/all_to_all | solution.py:221
  192.3 5.5 %all_to_all.133 = f32[2,1,65536]{2,1,0:T(1,128)S(1)} all-to-all(f32[2,1,65536]{2,1,0:T(1,128)S(1)} %reshape.617), channel_id=1, replica_groups=mesh['groups'=2,'vel'=8,'sub'=2] {'sub'}, dimensions={0} | all-to-all | bytes 1048576 | tf_op jit(solution)/shard_map/all_to_all | solution.py:220
  217.9 30.5 %psum.14 = f32[4,512]{1,0:T(4,128)} all-reduce(f32[4,512]{1,0:T(4,128)} %fusion.572), channel_id=1, replica_groups=mesh['groups'=2,'vel'=8,'sub'=2] {'vel','sub'}, use_global_device_ids=true, to_apply=%region_0.1 | all-reduce | flops 2048 | bytes 16384 | tf_op jit(solution)/shard_map/psum | solution.py:234
  254.5 4.1 slice_divide_fusion.5
  275.2 16.8 %all_to_all.134 = f32[8,1,16384]{2,1,0:T(1,128)S(1)} all-to-all(f32[8,1,16384]{2,1,0:T(1,128)S(1)} %reshape.619), channel_id=1, replica_groups=mesh['groups'=2,'vel'=8,'sub'=2] {'vel'}, dimensions={0} | all-to-all | bytes 1048576 | tf_op jit(solution)/shard_map/all_to_all | solution.py:210
  295.6 4.9 all_to_all.135
  312.4 3.7 subtract_bitcast_fusion.3
  371.1 3.6 fusion.54
  384.3 3.7 add_bitcast_fusion.2
  396.0 3.6 subtract_bitcast_fusion
  423.3 8.6 %fusion.2 = f32[16,16,16,32]{3,0,2,1:T(8,128)} fusion(f32[16,16,16,32]{3,0,2,1:T(8,128)S(1)} %bitcast.345, f32[16,16,32,16]{2,3,1,0:T(8,128)S(1)} %fusion.7, f32[16,16,32,16]{2,3,1,0:T(8,128)S(1)} %fusion.9, f32[16,16,32,16]{2,3,1,0:T(8,128)S(1)} %fusion.13, f32[16,16,32,16]{2,3,1,0:T(8,128)S(1)} %fusion.15, f32[16,16,32,16]{2,3,1,0:T(8,128)S(1)} %fusion.18, ...), kind=kLoop, calls=%fused_computation.5 | loop fusion | flops 1441792 | bytes 4194304 | tf_op jit(solution)/shard_map/add | solution.py:178
  434.4 17.0 %all_to_all.136 = f32[8,1,16384]{2,1,0:T(1,128)S(1)} all-to-all(f32[8,1,16384]{2,1,0:T(1,128)S(1)} %reshape.621), channel_id=1, replica_groups=mesh['groups'=2,'vel'=8,'sub'=2] {'vel'}, dimensions={0} | all-to-all | bytes 1048576 | tf_op jit(solution)/shard_map/all_to_all | solution.py:221
  458.4 5.5 %all_to_all.137 = f32[2,1,65536]{2,1,0:T(1,128)S(1)} all-to-all(f32[2,1,65536]{2,1,0:T(1,128)S(1)} %reshape.623), channel_id=1, replica_groups=mesh['groups'=2,'vel'=8,'sub'=2] {'sub'}, dimensions={0} | all-to-all | bytes 1048576 | tf_op jit(solution)/shard_map/all_to_all | solution.py:220
  481.6 29.9 %psum.15 = f32[4,512]{1,0:T(4,128)S(1)} all-reduce(f32[4,512]{1,0:T(4,128)S(1)} %fusion.571), channel_id=1, replica_groups=mesh['groups'=2,'vel'=8,'sub'=2] {'vel','sub'}, use_global_device_ids=true, to_apply=%region_6.8 | all-reduce | flops 2048 | bytes 16384 | tf_op jit(solution)/shard_map/psum | solution.py:234
  (267 shorter events, 336.1 us)
Async XLA Ops:
  1.8 11.1 %copy-start.33 = (s32[32]{0:T(128)S(1)}, s32[32]{0:T(128)}, u32[]{:S(2)}) copy-start(s32[32]{0:T(128)} %param.7) | copy-start | bytes 388
  1.8 11.1 %copy-start.12 = (s32[512]{0:T(512)S(1)}, s32[512]{0:T(512)}, u32[]{:S(2)}) copy-start(s32[512]{0:T(512)} %param.6) | copy-start | bytes 6148
  3.6 19.8 %all-to-all-start = ((f32[8,1,16384]{2,1,0:T(1,128)}), f32[8,1,16384]{2,1,0:T(1,128)S(1)}, u32[]{:S(2)}, u32[]{:S(2)}) async-start(f32[8,1,16384]{2,1,0:T(1,128)} %reshape.613), calls=%async_computation | async-start | bytes 1048576 | tf_op jit(solution)/shard_map/all_to_all | solution.py:210
  10.5 8.9 %copy-start.23 = (f32[8]{0:T(128)}, f32[8]{0:T(128)S(1)}, u32[]{:S(2)}) copy-start(f32[8]{0:T(128)S(1)} %get-tuple-element.71) | copy-start | bytes 100
  17.3 251.8 %copy-start.13 = (f32[512]{0:T(512)}, f32[512]{0:T(512)S(1)}, u32[]{:S(2)}) copy-start(f32[512]{0:T(512)S(1)} %sub.287) | copy-start | bytes 6148
  164.5 9.8 %copy-start.21 = (f32[496]{0:T(512)S(1)}, f32[496]{0:T(512)}, u32[]{:S(2)}) copy-start(f32[496]{0:T(512)} %get-tuple-element.55) | copy-start | bytes 5956
  164.5 9.8 %copy-start.22 = (f32[496]{0:T(512)S(1)}, f32[496]{0:T(512)}, u32[]{:S(2)}) copy-start(f32[496]{0:T(512)} %get-tuple-element.56) | copy-start | bytes 5956
  164.5 9.8 %copy-start.26 = (f32[16]{0:T(128)S(1)}, f32[16]{0:T(128)}, u32[]{:S(2)}) copy-start(f32[16]{0:T(128)} %get-tuple-element.53) | copy-start | bytes 196
  164.5 9.8 %copy-start.27 = (f32[16]{0:T(128)S(1)}, f32[16]{0:T(128)}, u32[]{:S(2)}) copy-start(f32[16]{0:T(128)} %get-tuple-element.54) | copy-start | bytes 196
  164.5 10.5 %copy-start.32 = (s32[32]{0:T(128)S(1)}, s32[32]{0:T(128)}, u32[]{:S(2)}) copy-start(s32[32]{0:T(128)} %get-tuple-element.11) | copy-start | bytes 388
  164.5 12.9 %copy-start.28 = (f32[8]{0:T(128)S(1)}, f32[8]{0:T(128)}, u32[]{:S(2)}) copy-start(f32[8]{0:T(128)} %get-tuple-element.72) | copy-start | bytes 100
  164.5 12.9 %copy-start.29 = (f32[32]{0:T(128)S(1)}, f32[32]{0:T(128)}, u32[]{:S(2)}) copy-start(f32[32]{0:T(128)} %get-tuple-element.63) | copy-start | bytes 388
  164.5 12.9 %copy-start.30 = (f32[32]{0:T(128)S(1)}, f32[32]{0:T(128)}, u32[]{:S(2)}) copy-start(f32[32]{0:T(128)} %get-tuple-element.64) | copy-start | bytes 388
  164.6 12.9 %copy-start.31 = (f32[32]{0:T(128)S(1)}, f32[32]{0:T(128)}, u32[]{:S(2)}) copy-start(f32[32]{0:T(128)} %get-tuple-element.68) | copy-start | bytes 388
  167.7 17.5 %all-to-all-start.2 = ((f32[8,1,16384]{2,1,0:T(1,128)}), f32[8,1,16384]{2,1,0:T(1,128)S(1)}, u32[]{:S(2)}, u32[]{:S(2)}) async-start(f32[8,1,16384]{2,1,0:T(1,128)} %reshape.615), calls=%async_computation.2 | async-start | bytes 1048576 | tf_op jit(solution)/shard_map/all_to_all | solution.py:221
  177.5 91.6 %copy-start.8 = (f32[8,32]{1,0:T(8,128)}, f32[8,32]{1,0:T(8,128)S(1)}, u32[]{:S(2)}) copy-start(f32[8,32]{1,0:T(8,128)S(1)} %get-tuple-element.57) | copy-start | bytes 3076
  177.5 91.6 %copy-start.10 = (f32[8,32]{1,0:T(8,128)}, f32[8,32]{1,0:T(8,128)S(1)}, u32[]{:S(2)}) copy-start(f32[8,32]{1,0:T(8,128)S(1)} %get-tuple-element.58) | copy-start | bytes 3076
  249.8 15.5 %copy-start.7 = (f32[256,496]{0,1:T(8,128)S(1)}, f32[256,496]{0,1:T(8,128)}, u32[]{:S(2)}) copy-start(f32[256,496]{0,1:T(8,128)} %get-tuple-element.33) | copy-start | bytes 1523716
  249.8 16.5 %copy-start.5 = (f32[256,511]{0,1:T(8,128)S(1)}, f32[256,511]{0,1:T(8,128)}, u32[]{:S(2)}) copy-start(f32[256,511]{0,1:T(8,128)} %get-tuple-element.30) | copy-start | bytes 1569796
  250.9 16.4 %copy-start.4 = (f32[256,511]{0,1:T(8,128)S(1)}, f32[256,511]{0,1:T(8,128)}, u32[]{:S(2)}) copy-start(f32[256,511]{0,1:T(8,128)} %get-tuple-element.31) | copy-start | bytes 1569796
  251.9 16.4 %collective-permute-start = (f32[8,32,32]{2,1,0:T(8,128)S(1)}, f32[8,32,32]{2,1,0:T(8,128)S(1)}, u32[]{:S(2)}, u32[]{:S(2)}) collective-permute-start(f32[8,32,32]{2,1,0:T(8,128)S(1)} %bitcast_select_fusion.1), channel_id=1, source_target_pairs={{0,1},{1,0},{2,3},{3,2},{4,5},{5,4},{6,7},{7,6},{8,9},{9,8},{10,11... | collective-permute-start | bytes 98312 | tf_op jit(solution)/shard_map/ppermute | solution.py:22
  479.6 32.0 %copy-start.16 = (f32[1,512]{1,0:T(1,128)S(1)}, f32[1,512]{1,0:T(1,128)}, u32[]{:S(2)}) copy-start(f32[1,512]{1,0:T(1,128)} %stack_reshape.3) | copy-start | bytes 6148
  479.6 36.1 %copy-start.25 = (pred[32]{0:T(512)(128)(4,1)S(1)}, pred[32]{0:T(512)(128)(4,1)}, u32[]{:S(2)}) copy-start(pred[32]{0:T(512)(128)(4,1)} %get-tuple-element.10) | copy-start | bytes 100
  515.7 9.2 %collective-permute-start.1 = (f32[8,32,32]{2,1,0:T(8,128)S(1)}, f32[8,32,32]{2,1,0:T(8,128)S(1)}, u32[]{:S(2)}, u32[]{:S(2)}) collective-permute-start(f32[8,32,32]{2,1,0:T(8,128)S(1)} %bitcast_select_fusion), channel_id=1, source_target_pairs={{0,1},{1,0},{2,3},{3,2},{4,5},{5,4},{6,7},{7,6},{8,9},{9,8},{10,11... | collective-permute-start | bytes 98312 | tf_op jit(solution)/shard_map/ppermute | solution.py:22
  (14 other events, 45.0 us)
where the time goes:
time: 535 us; the launch traced here: 529 us
  matrix products  244 us (46%)
  blocking collectives  116 us (22%)
  local copies, waits for them, and re-layouts  86.8 us (16%)
  other arithmetic  53.3 us (10%)
  starting transfers between devices  15.7 us (3%)
  waiting for transfers between devices  11.5 us (2%)
    dot_general x68, matrix products, apply(): return jnp.einsum(form, table, values, precision=HIGHEST)  212 us
    psum x2, blocking collectives, local(): flux = lax.psum(jnp.dot(weights, center, precision=HIGHEST), ('vel', 'sub'))  60.4 us
    unnamed x83, local copies, waits for them, and re-layouts  20 us
    add x2, other arithmetic, collide(): return cube + rate * (gain - cube * inverse(tables[2]))  17.1 us
    all_to_all x1, blocking collectives, local(): lax.all_to_all(post.reshape(count, count * count, 1, cells), 'vel', split...  17 us
    all_to_all x1, blocking collectives, local(): lax.all_to_all(state, 'vel', split_axis=2, concat_axis=1, tiled=True)  16.8 us
    dot_general x6, matrix products, inverse(): jnp.einsum(FORMS[2], cosine, second_real, precision=HIGHEST)  15.5 us
    dot_general x6, matrix products, inverse(): jnp.einsum(FORMS[2], sine_table, second_imag, precision=HIGHEST)  15 us
  transfers between devices with their start and end apart: 4, of which 2 were waited for; matrix products, arithmetic and copies ran while one was open for 7% of the time, Pallas kernels for 0%

commit v1 on v0

--- a/solution.py
+++ b/solution.py
@@ -231,7 +231,7 @@
             tiled=True,
         )
         center = back.reshape(local_y * local_xz, total_cells)
-        flux = lax.psum(jnp.dot(weights, center, precision=HIGHEST), ("vel", "sub"))
+        flux = lax.psum(lax.psum(jnp.dot(weights, center, precision=HIGHEST), "sub"), "vel")
         shaped = center.reshape(local_y, local_xz, total_cells)
         bottom_rows = jnp.take(shaped, bottom_index, axis=2)
         top_rows = shaped[:, :, height_count - 1 :: height_count]

time: 535 us -> 516 us (0.964)
  blocking collectives: 116 us -> 94.2 us
    psum x2 -> x4, blocking collectives: 60.4 us -> 38.7 us  [the longest x2 32.8 us: local(): lax.psum(lax.psum(jnp.dot(weights, center, precision=HIGHEST), 'sub'), 'v...]
where the time goes in v1:
time: 516 us; the launch traced here: 510 us
  matrix products  244 us (47%)
  blocking collectives  94.2 us (18%)
  local copies, waits for them, and re-layouts  86.7 us (17%)
  other arithmetic  53 us (10%)
  starting transfers between devices  18.4 us (4%)
  waiting for transfers between devices  11.9 us (2%)
    dot_general x68, matrix products, apply(): return jnp.einsum(form, table, values, precision=HIGHEST)  212 us
    psum x2, blocking collectives, local(): lax.psum(lax.psum(jnp.dot(weights, center, precision=HIGHEST), 'sub'), 'v...  32.8 us
    unnamed x83, local copies, waits for them, and re-layouts  20 us
    add x2, other arithmetic, collide(): return cube + rate * (gain - cube * inverse(tables[2]))  17.1 us
    all_to_all x1, blocking collectives, local(): lax.all_to_all(post.reshape(count, count * count, 1, cells), 'vel', split...  17 us
    all_to_all x1, blocking collectives, local(): lax.all_to_all(state, 'vel', split_axis=2, concat_axis=1, tiled=True)  16.8 us
    dot_general x6, matrix products, inverse(): jnp.einsum(FORMS[2], cosine, second_real, precision=HIGHEST)  15.5 us
    dot_general x6, matrix products, inverse(): jnp.einsum(FORMS[2], sine_table, second_imag, precision=HIGHEST)  15 us
  transfers between devices with their start and end apart: 4, of which 2 were waited for; matrix products, arithmetic and copies ran while one was open for 7% of the time, Pallas kernels for 0%

profile of v1, /device:TPU:1, one launch (start us, length us, event | category | flops | bytes accessed | tf_op | source)
XLA Modules:
  0.0 510.2 jit_solution(1484047886181224542)
XLA Ops:
  3.6 6.4 %all-to-all-start = ((f32[8,1,16384]{2,1,0:T(1,128)}), f32[8,1,16384]{2,1,0:T(1,128)S(1)}, u32[]{:S(2)}, u32[]{:S(2)}) async-start(f32[8,1,16384]{2,1,0:T(1,128)} %reshape.613), calls=%async_computation | async-start | bytes 1048576 | tf_op jit(solution)/shard_map/all_to_all | solution.py:210
  19.3 4.1 all-to-all-done
  27.6 5.8 %all_to_all.132 = f32[8,256,64]{1,0,2:T(8,128)S(1)} all-to-all(f32[8,256,64]{1,0,2:T(8,128)S(1)} %copy.780), channel_id=1, replica_groups=mesh['groups'=2,'vel'=8,'sub'=2] {'sub'}, dimensions={2} | all-to-all | bytes 1048576 | tf_op jit(solution)/shard_map/all_to_all | solution.py:209
  45.4 3.5 subtract_bitcast_fusion.7
  91.6 3.7 fusion.104
  128.7 3.8 subtract_bitcast_fusion.4
  156.1 8.6 %fusion.5 = f32[16,16,16,32]{3,0,2,1:T(8,128)} fusion(f32[16,16,16,32]{3,0,2,1:T(8,128)S(1)} %bitcast.348, f32[16,16,32,16]{2,3,1,0:T(8,128)S(1)} %fusion.23, f32[16,16,32,16]{2,3,1,0:T(8,128)S(1)} %fusion.25, f32[16,16,32,16]{2,3,1,0:T(8,128)S(1)} %fusion.29, f32[16,16,32,16]{2,3,1,0:T(8,128)S(1)} %fusion.31, f32[16,16,32,16]{2,3,1,0:T(8,128)S(1)} %fusion.34, ...), kind=kLoop, calls=%fused_computation.9 | loop fusion | flops 1441792 | bytes 4194304 | tf_op jit(solution)/shard_map/add | solution.py:178
  167.8 3.9 all-to-all-start.2
  177.5 7.9 %all-to-all-done.2 = f32[8,1,16384]{2,1,0:T(1,128)S(1)} async-done(((f32[8,1,16384]{2,1,0:T(1,128)}), f32[8,1,16384]{2,1,0:T(1,128)S(1)}, u32[]{:S(2)}, u32[]{:S(2)}) %all-to-all-start.2) | async-done | bytes 524320 | tf_op jit(solution)/shard_map/all_to_all | solution.py:221
  192.6 5.5 %all_to_all.133 = f32[2,1,65536]{2,1,0:T(1,128)S(1)} all-to-all(f32[2,1,65536]{2,1,0:T(1,128)S(1)} %reshape.617), channel_id=1, replica_groups=mesh['groups'=2,'vel'=8,'sub'=2] {'sub'}, dimensions={0} | all-to-all | bytes 1048576 | tf_op jit(solution)/shard_map/all_to_all | solution.py:220
  221.4 16.8 %psum.29 = f32[4,512]{1,0:T(4,128)} all-reduce(f32[4,512]{1,0:T(4,128)} %psum.28), channel_id=1, replica_groups=mesh['groups'=2,'vel'=8,'sub'=2] {'vel'}, use_global_device_ids=true, to_apply=%region_1.2 | all-reduce | flops 2048 | bytes 16384 | tf_op jit(solution)/shard_map/psum | solution.py:234
  241.7 3.9 collective-permute-start
  245.6 3.9 slice_divide_fusion.5
  266.1 16.8 %all_to_all.134 = f32[8,1,16384]{2,1,0:T(1,128)S(1)} all-to-all(f32[8,1,16384]{2,1,0:T(1,128)S(1)} %reshape.619), channel_id=1, replica_groups=mesh['groups'=2,'vel'=8,'sub'=2] {'vel'}, dimensions={0} | all-to-all | bytes 1048576 | tf_op jit(solution)/shard_map/all_to_all | solution.py:210
  286.5 4.9 all_to_all.135
  303.4 3.7 subtract_bitcast_fusion.3
  362.0 3.6 fusion.54
  375.2 3.7 add_bitcast_fusion.2
  386.9 3.6 subtract_bitcast_fusion
  414.2 8.6 %fusion.2 = f32[16,16,16,32]{3,0,2,1:T(8,128)} fusion(f32[16,16,16,32]{3,0,2,1:T(8,128)S(1)} %bitcast.345, f32[16,16,32,16]{2,3,1,0:T(8,128)S(1)} %fusion.7, f32[16,16,32,16]{2,3,1,0:T(8,128)S(1)} %fusion.9, f32[16,16,32,16]{2,3,1,0:T(8,128)S(1)} %fusion.13, f32[16,16,32,16]{2,3,1,0:T(8,128)S(1)} %fusion.15, f32[16,16,32,16]{2,3,1,0:T(8,128)S(1)} %fusion.18, ...), kind=kLoop, calls=%fused_computation.5 | loop fusion | flops 1441792 | bytes 4194304 | tf_op jit(solution)/shard_map/add | solution.py:178
  425.3 17.0 %all_to_all.136 = f32[8,1,16384]{2,1,0:T(1,128)S(1)} all-to-all(f32[8,1,16384]{2,1,0:T(1,128)S(1)} %reshape.621), channel_id=1, replica_groups=mesh['groups'=2,'vel'=8,'sub'=2] {'vel'}, dimensions={0} | all-to-all | bytes 1048576 | tf_op jit(solution)/shard_map/all_to_all | solution.py:221
  449.5 5.5 %all_to_all.137 = f32[2,1,65536]{2,1,0:T(1,128)S(1)} all-to-all(f32[2,1,65536]{2,1,0:T(1,128)S(1)} %reshape.623), channel_id=1, replica_groups=mesh['groups'=2,'vel'=8,'sub'=2] {'sub'}, dimensions={0} | all-to-all | bytes 1048576 | tf_op jit(solution)/shard_map/all_to_all | solution.py:220
  475.5 16.0 %psum.31 = f32[4,512]{1,0:T(4,128)S(1)} all-reduce(f32[4,512]{1,0:T(4,128)S(1)} %psum.30), channel_id=1, replica_groups=mesh['groups'=2,'vel'=8,'sub'=2] {'vel'}, use_global_device_ids=true, to_apply=%region_8.10 | all-reduce | flops 2048 | bytes 16384 | tf_op jit(solution)/shard_map/psum | solution.py:234
  495.4 4.2 collective-permute-start.1
  (269 shorter events, 343.5 us)
Async XLA Ops:
  1.8 11.0 %copy-start.33 = (s32[32]{0:T(128)S(1)}, s32[32]{0:T(128)}, u32[]{:S(2)}) copy-start(s32[32]{0:T(128)} %param.7) | copy-start | bytes 388
  1.8 11.0 %copy-start.12 = (s32[512]{0:T(512)S(1)}, s32[512]{0:T(512)}, u32[]{:S(2)}) copy-start(s32[512]{0:T(512)} %param.6) | copy-start | bytes 6148
  3.6 19.8 %all-to-all-start = ((f32[8,1,16384]{2,1,0:T(1,128)}), f32[8,1,16384]{2,1,0:T(1,128)S(1)}, u32[]{:S(2)}, u32[]{:S(2)}) async-start(f32[8,1,16384]{2,1,0:T(1,128)} %reshape.613), calls=%async_computation | async-start | bytes 1048576 | tf_op jit(solution)/shard_map/all_to_all | solution.py:210
  17.1 242.9 %copy-start.13 = (f32[512]{0:T(512)}, f32[512]{0:T(512)S(1)}, u32[]{:S(2)}) copy-start(f32[512]{0:T(512)S(1)} %sub.287) | copy-start | bytes 6148
  164.7 9.7 %copy-start.21 = (f32[496]{0:T(512)S(1)}, f32[496]{0:T(512)}, u32[]{:S(2)}) copy-start(f32[496]{0:T(512)} %get-tuple-element.55) | copy-start | bytes 5956
  164.7 9.7 %copy-start.22 = (f32[496]{0:T(512)S(1)}, f32[496]{0:T(512)}, u32[]{:S(2)}) copy-start(f32[496]{0:T(512)} %get-tuple-element.56) | copy-start | bytes 5956
  164.7 9.7 %copy-start.26 = (f32[16]{0:T(128)S(1)}, f32[16]{0:T(128)}, u32[]{:S(2)}) copy-start(f32[16]{0:T(128)} %get-tuple-element.53) | copy-start | bytes 196
  164.7 9.7 %copy-start.27 = (f32[16]{0:T(128)S(1)}, f32[16]{0:T(128)}, u32[]{:S(2)}) copy-start(f32[16]{0:T(128)} %get-tuple-element.54) | copy-start | bytes 196
  164.7 10.3 %copy-start.32 = (s32[32]{0:T(128)S(1)}, s32[32]{0:T(128)}, u32[]{:S(2)}) copy-start(s32[32]{0:T(128)} %get-tuple-element.11) | copy-start | bytes 388
  164.7 12.7 %copy-start.28 = (f32[8]{0:T(128)S(1)}, f32[8]{0:T(128)}, u32[]{:S(2)}) copy-start(f32[8]{0:T(128)} %get-tuple-element.72) | copy-start | bytes 100
  164.7 12.7 %copy-start.29 = (f32[32]{0:T(128)S(1)}, f32[32]{0:T(128)}, u32[]{:S(2)}) copy-start(f32[32]{0:T(128)} %get-tuple-element.63) | copy-start | bytes 388
  164.7 12.7 %copy-start.30 = (f32[32]{0:T(128)S(1)}, f32[32]{0:T(128)}, u32[]{:S(2)}) copy-start(f32[32]{0:T(128)} %get-tuple-element.64) | copy-start | bytes 388
  164.7 12.7 %copy-start.31 = (f32[32]{0:T(128)S(1)}, f32[32]{0:T(128)}, u32[]{:S(2)}) copy-start(f32[32]{0:T(128)} %get-tuple-element.68) | copy-start | bytes 388
  167.8 17.5 %all-to-all-start.2 = ((f32[8,1,16384]{2,1,0:T(1,128)}), f32[8,1,16384]{2,1,0:T(1,128)S(1)}, u32[]{:S(2)}, u32[]{:S(2)}) async-start(f32[8,1,16384]{2,1,0:T(1,128)} %reshape.615), calls=%async_computation.2 | async-start | bytes 1048576 | tf_op jit(solution)/shard_map/all_to_all | solution.py:221
  177.5 82.5 %copy-start.8 = (f32[8,32]{1,0:T(8,128)}, f32[8,32]{1,0:T(8,128)S(1)}, u32[]{:S(2)}) copy-start(f32[8,32]{1,0:T(8,128)S(1)} %get-tuple-element.57) | copy-start | bytes 3076
  177.5 82.5 %copy-start.10 = (f32[8,32]{1,0:T(8,128)}, f32[8,32]{1,0:T(8,128)S(1)}, u32[]{:S(2)}) copy-start(f32[8,32]{1,0:T(8,128)S(1)} %get-tuple-element.58) | copy-start | bytes 3076
  239.6 16.6 %copy-start.7 = (f32[256,496]{0,1:T(8,128)S(1)}, f32[256,496]{0,1:T(8,128)}, u32[]{:S(2)}) copy-start(f32[256,496]{0,1:T(8,128)} %get-tuple-element.33) | copy-start | bytes 1523716
  239.6 17.6 %copy-start.5 = (f32[256,511]{0,1:T(8,128)S(1)}, f32[256,511]{0,1:T(8,128)}, u32[]{:S(2)}) copy-start(f32[256,511]{0,1:T(8,128)} %get-tuple-element.30) | copy-start | bytes 1569796
  240.7 17.5 %copy-start.4 = (f32[256,511]{0,1:T(8,128)S(1)}, f32[256,511]{0,1:T(8,128)}, u32[]{:S(2)}) copy-start(f32[256,511]{0,1:T(8,128)} %get-tuple-element.31) | copy-start | bytes 1569796
  241.7 17.5 %collective-permute-start = (f32[8,32,32]{2,1,0:T(8,128)S(1)}, f32[8,32,32]{2,1,0:T(8,128)S(1)}, u32[]{:S(2)}, u32[]{:S(2)}) collective-permute-start(f32[8,32,32]{2,1,0:T(8,128)S(1)} %bitcast_select_fusion.1), channel_id=1, source_target_pairs={{0,1},{1,0},{2,3},{3,2},{4,5},{5,4},{6,7},{7,6},{8,9},{9,8},{10,11... | collective-permute-start | bytes 98312 | tf_op jit(solution)/shard_map/ppermute | solution.py:22
  470.7 20.8 %copy-start.16 = (f32[1,512]{1,0:T(1,128)S(1)}, f32[1,512]{1,0:T(1,128)}, u32[]{:S(2)}) copy-start(f32[1,512]{1,0:T(1,128)} %stack_reshape.3) | copy-start | bytes 6148
  470.7 24.7 %copy-start.25 = (pred[32]{0:T(512)(128)(4,1)S(1)}, pred[32]{0:T(512)(128)(4,1)}, u32[]{:S(2)}) copy-start(pred[32]{0:T(512)(128)(4,1)} %get-tuple-element.10) | copy-start | bytes 100
  495.3 9.5 %copy-start.2 = (f32[256,511]{0,1:T(8,128)S(1)}, f32[256,511]{0,1:T(8,128)}, u32[]{:S(2)}) copy-start(f32[256,511]{0,1:T(8,128)} %get-tuple-element.25) | copy-start | bytes 1569796
  495.4 10.5 %collective-permute-start.1 = (f32[8,32,32]{2,1,0:T(8,128)S(1)}, f32[8,32,32]{2,1,0:T(8,128)S(1)}, u32[]{:S(2)}, u32[]{:S(2)}) collective-permute-start(f32[8,32,32]{2,1,0:T(8,128)S(1)} %bitcast_select_fusion), channel_id=1, source_target_pairs={{0,1},{1,0},{2,3},{3,2},{4,5},{5,4},{6,7},{7,6},{8,9},{9,8},{10,11... | collective-permute-start | bytes 98312 | tf_op jit(solution)/shard_map/ppermute | solution.py:22
  (14 other events, 48.0 us)
